TPU v7x, 32 devices: a whole 2x2x4 slice. The times are simulated.
32 devices in a mesh: pb: 8 (over z, x), ao: 4 (over y, core).
Axes of the slice: x: 2, y: 2, z: 4, core: 2. Of those that a mesh axis runs over, the one named last changes fastest.
Arguments:
- queries: bfloat16 [8192, 128], P('pb'), may hold values from -4 to 4
- centres: bfloat16 [8192, 128], P(('pb', 'ao')), may hold values from -4 to 4
- coefs: bfloat16 [8192, 4096], P('pb', 'ao'), may hold values from -3 to 3
- pattern: int32 [8, 5], replicated, may hold values from 0 to 1, as said below
Outputs:
- scores: bfloat16 [8192, 4096], P('pb', 'ao')
Inputs may be any that keep to these rules, and one draw needn't show every extreme that they name: pattern[i, j] tells whether query block i lists centre block i + j - 2; it is 0 where that block lies outside 0 to 7, and 1 for j = 2.
All inputs are finite; a program needn't handle non-finite values.
Results may differ from a plain program's by a relative error of at most 0.0049.
Values may be sent and summed in bfloat16 or wider, within the bound.
No kernel may reach another device: no remote copies, remote signals or barrier semaphores. Data moves between devices by JAX's collectives and lax.ppermute only.
A program may use at most 64 MiB of HBM per device.

v0:
```python
import functools
import math

import jax
import jax.numpy as jnp
from jax import lax
from jax.experimental import pallas as pl
from jax.experimental.pallas import tpu as pltpu
from jax.sharding import PartitionSpec as P

RADIUS_FACTOR = 1.3
VMEM_LIMIT = 24 * 1024 * 1024
BF16 = jnp.bfloat16
F32 = jnp.float32
SMEM = pl.BlockSpec(memory_space=pltpu.SMEM)
WHOLE = pl.BlockSpec(memory_space=pltpu.VMEM)
ANY = pl.BlockSpec(memory_space=pl.ANY)


COST = pl.CostEstimate(flops=1 << 20, bytes_accessed=1 << 16, transcendentals=0)


def three_terms(norm):
    high = norm.astype(BF16).astype(F32)
    middle = (norm - high).astype(BF16).astype(F32)
    return high, middle, norm - high - middle


def widened(rows, centre_side):
    wide = rows.astype(F32)
    high, middle, low = three_terms(jnp.sum(wide * wide, axis=1, keepdims=True))
    lane = lax.broadcasted_iota(jnp.int32, (rows.shape[0], 128), 1)
    first, ones = (3, 0) if centre_side else (0, 3)
    extra = jnp.where((lane >= ones) & (lane < ones + 3), 1.0, 0.0)
    extra = jnp.where(lane == first, high, extra)
    extra = jnp.where(lane == first + 1, middle, extra)
    extra = jnp.where(lane == first + 2, low, extra)
    own = (wide * -2.0).astype(BF16) if centre_side else rows
    return jnp.concatenate([own, extra.astype(BF16)], axis=1)


def in_vmem(*arrays):
    return [pltpu.with_memory_space_constraint(array, pltpu.VMEM) for array in arrays]


def cut_kernel(radius, pairs, place_ref, pattern_ref, out_ref):
    me, core = place_ref[0], place_ref[1]
    side = 1 - 2 * lax.rem(me, 2)
    blocks, band = pattern_ref.shape
    for k, pair in enumerate(pairs):
        query_block, centre_block = (me + side * jnp.where(core == 0, step[0], step[1]) for step in pair)
        query_block = jnp.clip(query_block, 0, blocks - 1)
        offset = jnp.clip(centre_block - query_block + band // 2, 0, band - 1)
        cut = jnp.where(pattern_ref[query_block, offset] > 0, jnp.float32(radius), jnp.float32(-1.0))
        out_ref[k] = jnp.full(out_ref.shape[1:], cut, F32)


def cut_values(place, pattern, pairs, radius):
    return pl.pallas_call(
        functools.partial(cut_kernel, radius, pairs),
        in_specs=[SMEM, SMEM],
        out_specs=WHOLE,
        out_shape=pltpu.VMEM((len(pairs), 8, 256), F32),
        compiler_params=pltpu.CompilerParams(vmem_limit_bytes=VMEM_LIMIT),
        cost_estimate=COST,
        name="cuts",
    )(place, pattern)


def kern_tile(query, centre_wide, cut_ref, radius, out_ref, column):
    depth = centre_wide.shape[0]
    columns = min(256, depth)
    for start in range(0, depth, columns):
        square = lax.dot_general(
            query, centre_wide[pl.ds(start, columns), :], (((1,), (1,)), ((), ())), preferred_element_type=F32
        )
        square = jnp.maximum(square, 1e-30)
        dist = square * lax.rsqrt(square)
        inner = jnp.maximum(cut_ref[:1, :columns] - dist, 0.0)
        inner = inner * inner
        out_ref[:, pl.ds(column + start, columns)] = (inner * inner * (dist + radius / 4)).astype(BF16)


def kern_kernel(radius, cuts, sources, scored, carried, cut_ref, query_ref, *refs):
    blocks = len(cuts)
    centres, refs = refs[: blocks * sources], refs[blocks * sources :]
    coefs, refs = refs[: blocks * scored], refs[blocks * scored :]
    carry, refs = refs[:carried], refs[carried:]
    out_ref, *carry_out = refs[: 1 + carried]
    query_wide, centre_wide, *scratch = refs[1 + carried :]
    copies = []
    if scored:
        kern_ref, coef_ref, sems = scratch
        depth = centre_wide.shape[1]
        for b, coef in enumerate(coefs):
            copies.append(pltpu.make_async_copy(coef, coef_ref.at[pl.ds(b * depth, depth), :], sems.at[b]))
        for source, target in zip(carry, carry_out):
            copies.append(pltpu.make_async_copy(source, target, sems.at[blocks]))
    for copy in copies:
        copy.start()

    query_wide[...] = widened(query_ref[...], False)
    for b in range(blocks):
        centre = centres[b * sources][...]
        for source in centres[b * sources + 1 : (b + 1) * sources]:
            centre = centre + source[...]
        centre_wide[b] = widened(centre, True)

    tile = min(512, query_wide.shape[0])
    for row in range(query_wide.shape[0] // tile):
        rows = pl.ds(row * tile, tile)
        values = kern_ref if scored else out_ref.at[rows, :]
        for b, cut in enumerate(cuts):
            kern_tile(query_wide[rows, :], centre_wide.at[b], cut_ref.at[cut], radius, values, b * centre_wide.shape[1])
        if row == 0:
            for copy in copies:
                copy.wait()
        if scored:
            total = jnp.dot(kern_ref[...], coef_ref[...], preferred_element_type=F32)
            out_ref[rows, :] = total.astype(out_ref.dtype)


def kern_blocks(cut_rows, queries, centres, cuts, coefs=(), dtype=BF16, carry=()):
    query_rows, features = queries.shape
    blocks, centre_rows = len(centres), centres[0][0].shape[0]
    scratch = [
        pltpu.VMEM((query_rows, features + 128), BF16),
        pltpu.VMEM((blocks, centre_rows, features + 128), BF16),
    ]
    out_shape = [pltpu.VMEM((query_rows, blocks * centre_rows), BF16)]
    if coefs:
        width = coefs[0].shape[1]
        out_shape = [pltpu.VMEM((query_rows, width), dtype)]
        scratch += [
            pltpu.VMEM((min(512, query_rows), blocks * centre_rows), BF16),
            pltpu.VMEM((blocks * centre_rows, width), BF16),
            pltpu.SemaphoreType.DMA((blocks + 1,)),
        ]
    out_shape += [pltpu.VMEM(array.shape, array.dtype) for array in carry]
    pieces = [source for block in centres for source in block]
    out = pl.pallas_call(
        functools.partial(
            kern_kernel, RADIUS_FACTOR * math.sqrt(features), cuts, len(centres[0]), len(coefs) > 0, len(carry)
        ),
        in_specs=[WHOLE] * (2 + len(pieces)) + [ANY] * (len(coefs) + len(carry)),
        out_specs=[WHOLE] * len(out_shape),
        out_shape=out_shape,
        scratch_shapes=scratch,
        compiler_params=pltpu.CompilerParams(vmem_limit_bytes=VMEM_LIMIT),
        cost_estimate=COST,
        name="kern",
    )(cut_rows, queries, *pieces, *coefs, *carry)
    return out if carry else out[0]


def score_sum(terms, kern_refs, coef_refs, rows):
    total = None
    for kern, block, coef, column, width in terms:
        depth = coef_refs[coef].shape[0]
        product = jnp.dot(
            kern_refs[kern][rows, pl.ds(block * depth, depth)],
            coef_refs[coef][:, pl.ds(column, width)],
            preferred_element_type=F32,
        )
        total = product if total is None else total + product
    return total


def score_kernel(terms, kerns, adds, column, tile, *refs):
    out_ref = refs[-1]
    coefs = refs[kerns : len(refs) - 1 - adds]

    @pl.loop(0, out_ref.shape[0] // tile)
    def _(row):
        rows = pl.ds(pl.multiple_of(row * tile, tile), tile)
        total = score_sum(terms, refs[:kerns], coefs, rows)
        if adds:
            total = total + refs[-2][rows, pl.ds(column, total.shape[1])].astype(F32)
        out_ref[rows, :] = total.astype(out_ref.dtype)


def scores(kerns, coefs, terms, dtype, add=None, column=0):
    rows, width = kerns[0].shape[0], terms[0][4]
    adds = [] if add is None else [add]
    return pl.pallas_call(
        functools.partial(score_kernel, terms, len(kerns), len(adds), column, min(256, rows)),
        in_specs=[WHOLE] * (len(kerns) + len(coefs) + len(adds)),
        out_specs=WHOLE,
        out_shape=pltpu.VMEM((rows, width), dtype),
        compiler_params=pltpu.CompilerParams(vmem_limit_bytes=VMEM_LIMIT),
        cost_estimate=COST,
        name="scores",
    )(*in_vmem(*kerns, *coefs, *adds))


def far_kernel(tile, place_ref, kern_ref, far_0_ref, far_1_ref, add_ref, out_ref):
    def sums(coef_ref):
        @pl.loop(0, out_ref.shape[0] // tile)
        def _(row):
            rows = pl.ds(pl.multiple_of(row * tile, tile), tile)
            total = jnp.dot(kern_ref[rows, :], coef_ref[...], preferred_element_type=F32)
            out_ref[rows, :] = total + add_ref[rows, :]

    @pl.when(place_ref[1] == 0)
    def _():
        sums(far_0_ref)

    @pl.when(place_ref[1] == 1)
    def _():
        sums(far_1_ref)


def far_sum(place, kern, far_0, far_1, add):
    rows = kern.shape[0]
    return pl.pallas_call(
        functools.partial(far_kernel, min(256, rows)),
        in_specs=[SMEM] + [WHOLE] * 4,
        out_specs=WHOLE,
        out_shape=pltpu.VMEM(add.shape, add.dtype),
        input_output_aliases={4: 0},
        compiler_params=pltpu.CompilerParams(vmem_limit_bytes=VMEM_LIMIT),
        cost_estimate=COST,
        name="far",
    )(place, *in_vmem(kern, far_0, far_1, add))


def final_kernel(scale, tile, column, add_ref, part_ref, *refs):
    out_ref = refs[-1]
    rows = pl.ds(pl.multiple_of(pl.program_id(0) * tile, tile), tile)
    total = part_ref[rows, :].astype(F32) + add_ref[rows, pl.ds(column, out_ref.shape[1])]
    out_ref[...] = (total * scale).astype(out_ref.dtype)


def final(add, part, scale, half, halves, out):
    rows, width = part.shape
    tile = min(512, rows)
    return pl.pallas_call(
        functools.partial(final_kernel, scale, tile, half * width),
        grid=(rows // tile,),
        in_specs=[WHOLE] * 2 + ([] if out is None else [ANY]),
        out_specs=pl.BlockSpec((tile, width), lambda r: (r, half)),
        out_shape=jax.ShapeDtypeStruct((rows, width * halves), BF16),
        input_output_aliases={} if out is None else {2: 0},
        compiler_params=pltpu.CompilerParams(vmem_limit_bytes=VMEM_LIMIT),
        cost_estimate=COST,
        name="final",
    )(*in_vmem(add, part), *([] if out is None else [out]))


def after(array, *others):
    return lax.optimization_barrier((array, *others))[0]


def per_device(queries, centres, coefs, pattern):
    blocks, members = lax.axis_size("pb"), lax.axis_size("ao")
    radius = RADIUS_FACTOR * math.sqrt(queries.shape[1])
    me, core = lax.axis_index("pb"), lax.rem(lax.axis_index("ao"), 2)
    place = jnp.stack([me, core])

    def send(block, *targets):
        route = []
        for i in range(blocks):
            for m in range(members):
                target = targets[m % 2](i)
                if target is not None and 0 <= target[0] < blocks:
                    route.append((i * members + m, target[0] * members + m // 2 * 2 + target[1]))
        return lax.ppermute(block, ("pb", "ao"), route)

    sign = lambda i: 1 - 2 * (i % 2)
    partner = lambda c: lambda i: (i + sign(i), c)
    front = lambda c: lambda i: (i + 2 * sign(i), c)
    back = lambda c: lambda i: (i - 2 * sign(i), c)
    nobody = lambda i: None

    near = send(coefs, partner(0), back(1))
    query_t = send(queries, back(0), partner(1))
    far_1 = send(coefs, nobody, front(1))
    centre_own = lax.all_gather(centres, "ao", axis=0, tiled=True)
    centre_near = send(after(centre_own, query_t), back(1), partner(0))

    at_me, at_target, at_near, at_far = (0, 0), (2, 1), (1, 2), (2, -2)
    pairs = ((at_target, at_me), (at_target, at_near), (at_me, at_me), (at_me, at_near), (at_me, at_far))
    cut_rows = cut_values(place, pattern, pairs, radius)

    def kern(order, queries, query_at, centres, at, *scored):
        cuts = tuple(pairs.index((query_at, centre_at)) for centre_at in at)
        return kern_blocks(after(cut_rows, *order), queries, centres, cuts, *scored)

    width = coefs.shape[1] // 2
    coefs_hbm = pltpu.with_memory_space_constraint(coefs, pltpu.HBM)
    base_t = kern((), query_t, at_target, [[centre_own]], [at_me], [coefs_hbm])
    centre_far_1 = send(after(centre_own, base_t), nobody, front(1))
    kern_t = kern((base_t,), query_t, at_target, [[centre_near]], [at_near])
    far_0 = send(after(coefs, kern_t), back(0), nobody)
    near = after(near, kern_t)
    total, part = [], []
    for h in range(2):
        if h == 1:
            near = after(near, total[0], far_1, centre_far_1)
        total.append(scores([kern_t], [near], ((0, 0, 0, h * width, width),), BF16, base_t, h * width))
        part.append(send(total[h], front(0), partner(1)))
    centre_far_0 = send(after(centre_near, total[1]), nobody, lambda i: (i, 0))
    own, far_1 = kern(
        (total[1],), queries, at_me, [[centre_own], [centre_near]], [at_me, at_near], [coefs_hbm, near], F32, [far_1]
    )
    kern_far = kern((own,), queries, at_me, [[centre_far_0, centre_far_1]], [at_far])
    own = far_sum(place, kern_far, far_0, far_1, own)

    scale = 4.0 / radius**5
    out = None
    for h in range(2):
        out = final(own, part[h], scale, h, 2, out)
    return out


def solution(mesh):
    in_specs = (P("pb", None), P(("pb", "ao"), None), P("pb", "ao"), P())
    out_specs = P("pb", "ao")
    return jax.shard_map(
        per_device, mesh=mesh, in_specs=in_specs, out_specs=out_specs, check_vma=False
    )
```

profile of v0, /device:TPU:0, one launch (start us, length us, event | category | flops | bytes accessed | tf_op | source)
XLA Modules:
  0.0 65.2 jit_solution(4171447332394317636)
XLA Ops:
  0.0 4.8 %collective-permute-start.2 = (bf16[1024,1024]{1,0:T(8,128)(2,1)}, bf16[1024,1024]{1,0:T(8,128)(2,1)S(1)}, u32[]{:S(2)}, u32[]{:S(2)}) collective-permute-start(bf16[1024,1024]{1,0:T(8,128)(2,1)} %refs_2_.1), channel_id=1, source_target_pairs={{0,4},{2,6},{4,0},{5,13},{6,2},{7,15},{8,12},{9,1},{10,14},{11,3},... | collective-permute-start | bytes 6291464 | tf_op jit(solution)/shard_map/ppermute | solution.py:267
  4.8 2.0 %collective-permute-start.3 = (bf16[1024,1024]{1,0:T(8,128)(2,1)}, bf16[1024,1024]{1,0:T(8,128)(2,1)}, u32[]{:S(2)}, u32[]{:S(2)}) collective-permute-start(bf16[1024,1024]{1,0:T(8,128)(2,1)} %refs_2_.1), channel_id=1, source_target_pairs={{1,9},{3,11},{9,17},{11,19},{13,5},{15,7},{17,25},{19,27},{21,13},... | collective-permute-start | bytes 6291464 | tf_op jit(solution)/shard_map/ppermute | solution.py:267
  6.8 1.3 %collective-permute-start = (bf16[1024,128]{1,0:T(8,128)(2,1)}, bf16[1024,128]{1,0:T(8,128)(2,1)S(1)}, u32[]{:S(2)}, u32[]{:S(2)}) collective-permute-start(bf16[1024,128]{1,0:T(8,128)(2,1)} %query_ref.3), channel_id=1, source_target_pairs={{1,5},{3,7},{4,12},{5,1},{6,14},{7,3},{8,0},{9,13},{10,2},{11,15},... | collective-permute-start | bytes 786440 | tf_op jit(solution)/shard_map/ppermute | solution.py:267
  8.1 7.3 %all_gather.3.refs_0_ = bf16[1024,128]{1,0:T(8,128)(2,1)S(1)} all-gather(bf16[256,128]{1,0:T(8,128)(2,1)} %param.5), channel_id=1, replica_groups=mesh['pb'=8,'ao'=4] {'ao'}, dimensions={0}, use_global_device_ids=true | all-gather | bytes 327680 | tf_op jit(solution)/shard_map/all_gather | solution.py:278
  15.4 2.8 %collective-permute-done.query_ref = bf16[1024,128]{1,0:T(8,128)(2,1)S(1)} collective-permute-done((bf16[1024,128]{1,0:T(8,128)(2,1)}, bf16[1024,128]{1,0:T(8,128)(2,1)S(1)}, u32[]{:S(2)}, u32[]{:S(2)}) %collective-permute-start) | collective-permute-done | bytes 262176 | tf_op jit(solution)/shard_map/ppermute | solution.py:267
  18.2 1.3 %collective-permute-start.1 = (bf16[1024,128]{1,0:T(8,128)(2,1)S(1)}, bf16[1024,128]{1,0:T(8,128)(2,1)S(1)}, u32[]{:S(2)}, u32[]{:S(2)}) collective-permute-start(bf16[1024,128]{1,0:T(8,128)(2,1)S(1)} %all_gather.3.refs_0_), channel_id=1, source_target_pairs={{1,4},{3,6},{4,13},{5,0},{6,15},{7,2},{8,1},{9,12},{10,3},{11,14},... | collective-permute-start | bytes 786440 | tf_op jit(solution)/shard_map/ppermute | solution.py:267
  19.5 0.1 pad_add_fusion.place_ref
  19.6 0.0 copy-start.1
  19.6 0.7 %copy-done.1 = s32[8,5]{1,0:T(8,128)S(1)} copy-done((s32[8,5]{1,0:T(8,128)S(1)}, s32[8,5]{1,0:T(8,128)}, u32[]{:S(2)}) %copy-start.1) | copy-done | bytes 184
  20.2 0.6 cuts.1.cut_ref
  20.9 4.6 %kern.4.refs_2_ = bf16[1024,1024]{1,0:T(8,128)(2,1)S(1)} custom-call(f32[5,8,256]{2,1,0:T(8,128)S(1)} %cuts.1.cut_ref, bf16[1024,128]{1,0:T(8,128)(2,1)S(1)} %collective-permute-done.query_ref, bf16[1024,128]{1,0:T(8,128)(2,1)S(1)} %all_gather.3.refs_0_, bf16[1024,1024]{1,0:T(8,128)(2,1)} %refs_2_.1), custom_call_target="tpu_custom_call" | custom-call | flops 1048576 | bytes 65536 | tf_op jit(solution)/shard_map/kern/pallas_call | solution.py:141
  25.5 0.0 copy-start.2
  25.5 3.3 %collective-permute-done.1.refs_0_.refs_1_ = bf16[1024,128]{1,0:T(8,128)(2,1)S(1)} collective-permute-done((bf16[1024,128]{1,0:T(8,128)(2,1)S(1)}, bf16[1024,128]{1,0:T(8,128)(2,1)S(1)}, u32[]{:S(2)}, u32[]{:S(2)}) %collective-permute-start.1) | collective-permute-done | bytes 262176 | tf_op jit(solution)/shard_map/ppermute | solution.py:267
  28.7 2.0 %kern.5.refs_0_ = bf16[1024,1024]{1,0:T(8,128)(2,1)S(1)} custom-call(f32[5,8,256]{2,1,0:T(8,128)S(1)} %cuts.1.cut_ref, bf16[1024,128]{1,0:T(8,128)(2,1)S(1)} %collective-permute-done.query_ref, bf16[1024,128]{1,0:T(8,128)(2,1)S(1)} %collective-permute-done.1.refs_0_.refs_1_), custom_call_target="tpu_custom_call" | custom-call | flops 1048576 | bytes 65536 | tf_op jit(solution)/shard_map/kern/pallas_call | solution.py:141
  30.8 0.0 copy-done.2
  30.8 1.3 %collective-permute-start.6 = (bf16[1024,1024]{1,0:T(8,128)(2,1)S(1)}, bf16[1024,1024]{1,0:T(8,128)(2,1)S(1)}, u32[]{:S(2)}, u32[]{:S(2)}) collective-permute-start(bf16[1024,1024]{1,0:T(8,128)(2,1)S(1)} %copy-done.2), channel_id=1, source_target_pairs={{4,12},{6,14},{8,0},{10,2},{12,20},{14,22},{16,8},{18,10},{20,28},... | collective-permute-start | bytes 6291464 | tf_op jit(solution)/shard_map/ppermute | solution.py:267
  32.1 0.7 %collective-permute-start.4 = (bf16[1024,128]{1,0:T(8,128)(2,1)S(1)}, bf16[1024,128]{1,0:T(8,128)(2,1)S(1)}, u32[]{:S(2)}, u32[]{:S(2)}) collective-permute-start(bf16[1024,128]{1,0:T(8,128)(2,1)S(1)} %all_gather.3.refs_0_), channel_id=1, source_target_pairs={{1,9},{3,11},{9,17},{11,19},{13,5},{15,7},{17,25},{19,27},{21,13},... | collective-permute-start | bytes 786440 | tf_op jit(solution)/shard_map/ppermute | solution.py:267
  32.8 1.9 %collective-permute-done.2.refs_1_.refs_3_ = bf16[1024,1024]{1,0:T(8,128)(2,1)S(1)} collective-permute-done((bf16[1024,1024]{1,0:T(8,128)(2,1)}, bf16[1024,1024]{1,0:T(8,128)(2,1)S(1)}, u32[]{:S(2)}, u32[]{:S(2)}) %collective-permute-start.2) | collective-permute-done | bytes 2097184 | tf_op jit(solution)/shard_map/ppermute | solution.py:267
  34.7 1.8 %scores.2 = bf16[1024,512]{1,0:T(8,128)(2,1)S(1)} custom-call(bf16[1024,1024]{1,0:T(8,128)(2,1)S(1)} %kern.5.refs_0_, bf16[1024,1024]{1,0:T(8,128)(2,1)S(1)} %collective-permute-done.2.refs_1_.refs_3_, bf16[1024,1024]{1,0:T(8,128)(2,1)S(1)} %kern.4.refs_2_), custom_call_target="tpu_custom_call" | custom-call | flops 1048576 | bytes 65536 | tf_op jit(solution)/shard_map/scores/pallas_call | solution.py:185
  36.4 0.0 copy-start
  36.4 4.2 %collective-permute-start.8 = (bf16[1024,512]{1,0:T(8,128)(2,1)S(1)}, bf16[1024,512]{1,0:T(8,128)(2,1)S(1)}, u32[]{:S(2)}, u32[]{:S(2)}) collective-permute-start(bf16[1024,512]{1,0:T(8,128)(2,1)S(1)} %scores.2), channel_id=1, source_target_pairs={{0,8},{1,5},{2,10},{3,7},{5,1},{7,3},{8,16},{9,13},{10,18},{11,15}... | collective-permute-start | bytes 3145736 | tf_op jit(solution)/shard_map/ppermute | solution.py:267
  40.7 0.0 collective-permute-done.4.refs_1_
  40.7 0.0 collective-permute-done.3.refs_4_
  40.7 1.8 %scores.3 = bf16[1024,512]{1,0:T(8,128)(2,1)S(1)} custom-call(bf16[1024,1024]{1,0:T(8,128)(2,1)S(1)} %kern.5.refs_0_, bf16[1024,1024]{1,0:T(8,128)(2,1)S(1)} %collective-permute-done.2.refs_1_.refs_3_, bf16[1024,1024]{1,0:T(8,128)(2,1)S(1)} %kern.4.refs_2_), custom_call_target="tpu_custom_call" | custom-call | flops 1048576 | bytes 65536 | tf_op jit(solution)/shard_map/scores/pallas_call | solution.py:185
  42.4 3.5 %collective-permute-start.7 = (bf16[1024,512]{1,0:T(8,128)(2,1)S(1)}, bf16[1024,512]{1,0:T(8,128)(2,1)S(1)}, u32[]{:S(2)}, u32[]{:S(2)}) collective-permute-start(bf16[1024,512]{1,0:T(8,128)(2,1)S(1)} %scores.3), channel_id=1, source_target_pairs={{0,8},{1,5},{2,10},{3,7},{5,1},{7,3},{8,16},{9,13},{10,18},{11,15}... | collective-permute-start | bytes 3145736 | tf_op jit(solution)/shard_map/ppermute | solution.py:267
  45.9 1.5 %collective-permute-start.5 = (bf16[1024,128]{1,0:T(8,128)(2,1)S(1)}, bf16[1024,128]{1,0:T(8,128)(2,1)S(1)}, u32[]{:S(2)}, u32[]{:S(2)}) collective-permute-start(bf16[1024,128]{1,0:T(8,128)(2,1)S(1)} %collective-permute-done.1.refs_0_.refs_1_), channel_id=1, source_target_pairs={{1,0},{3,2},{5,4},{7,6},{9,8},{11,10},{13,12},{15,14},{17,16},{19,... | collective-permute-start | bytes 786440 | tf_op jit(solution)/shard_map/ppermute | solution.py:267
  47.4 0.0 copy-done
  47.4 7.9 %kern.6 = (f32[1024,1024]{1,0:T(8,128)S(1)}, bf16[1024,1024]{1,0:T(8,128)(2,1)S(1)}) custom-call(f32[5,8,256]{2,1,0:T(8,128)S(1)} %cuts.1.cut_ref, bf16[1024,128]{1,0:T(8,128)(2,1)S(1)} %copy-done, bf16[1024,128]{1,0:T(8,128)(2,1)S(1)} %all_gather.3.refs_0_, bf16[1024,128]{1,0:T(8,128)(2,1)S(1)} %collective-permute-done.1.refs_0_.refs_1_, ...), custom_call_target="tpu_custom_call" | custom-call | flops 1048576 | bytes 65536 | tf_op jit(solution)/shard_map/kern/pallas_call | solution.py:141
  55.3 0.0 collective-permute-done.5.refs_0_
  55.3 2.1 %kern.7.kern_ref = bf16[1024,1024]{1,0:T(8,128)(2,1)S(1)} custom-call(f32[5,8,256]{2,1,0:T(8,128)S(1)} %cuts.1.cut_ref, bf16[1024,128]{1,0:T(8,128)(2,1)S(1)} %copy-done, bf16[1024,128]{1,0:T(8,128)(2,1)S(1)} %collective-permute-done.5.refs_0_, bf16[1024,128]{1,0:T(8,128)(2,1)S(1)} %collective-permute-done.4.refs_1_), custom_call_target="tpu_custom_call" | custom-call | flops 1048576 | bytes 65536 | tf_op jit(solution)/shard_map/kern/pallas_call | solution.py:141
  57.4 1.3 %collective-permute-done.6.far_0_ref = bf16[1024,1024]{1,0:T(8,128)(2,1)S(1)} collective-permute-done((bf16[1024,1024]{1,0:T(8,128)(2,1)S(1)}, bf16[1024,1024]{1,0:T(8,128)(2,1)S(1)}, u32[]{:S(2)}, u32[]{:S(2)}) %collective-permute-start.6) | collective-permute-done | bytes 2097184 | tf_op jit(solution)/shard_map/ppermute | solution.py:267
  58.7 3.4 %far.1.add_ref = f32[1024,1024]{1,0:T(8,128)S(1)} custom-call(s32[2]{0:T(128)S(1)} %pad_add_fusion.place_ref, bf16[1024,1024]{1,0:T(8,128)(2,1)S(1)} %kern.7.kern_ref, bf16[1024,1024]{1,0:T(8,128)(2,1)S(1)} %collective-permute-done.6.far_0_ref, bf16[1024,1024]{1,0:T(8,128)(2,1)S(1)} %get-tuple-element.26.far_1_ref, ...), custom_call_target="tpu_custom_call", output_to_operand_aliasing={{}: (4, {})} | custom-call | flops 1048576 | bytes 65536 | tf_op jit(solution)/shard_map/far/pallas_call | solution.py:215
  62.2 0.0 collective-permute-done.8.part_ref
  62.2 1.1 %final.2.refs_0_ = bf16[1024,1024]{1,0:T(8,128)(2,1)} custom-call(f32[1024,1024]{1,0:T(8,128)S(1)} %far.1.add_ref, bf16[1024,512]{1,0:T(8,128)(2,1)S(1)} %collective-permute-done.8.part_ref), custom_call_target="tpu_custom_call" | custom-call | flops 1048576 | bytes 65536 | tf_op jit(solution)/shard_map/final/pallas_call | solution.py:237
  63.3 0.8 %collective-permute-done.7.part_ref = bf16[1024,512]{1,0:T(8,128)(2,1)S(1)} collective-permute-done((bf16[1024,512]{1,0:T(8,128)(2,1)S(1)}, bf16[1024,512]{1,0:T(8,128)(2,1)S(1)}, u32[]{:S(2)}, u32[]{:S(2)}) %collective-permute-start.7) | collective-permute-done | bytes 1048608 | tf_op jit(solution)/shard_map/ppermute | solution.py:267
  64.1 1.1 %final.3 = bf16[1024,1024]{1,0:T(8,128)(2,1)} custom-call(f32[1024,1024]{1,0:T(8,128)S(1)} %far.1.add_ref, bf16[1024,512]{1,0:T(8,128)(2,1)S(1)} %collective-permute-done.7.part_ref, bf16[1024,1024]{1,0:T(8,128)(2,1)} %final.2.refs_0_), custom_call_target="tpu_custom_call", output_to_operand_aliasing={{}: (2, {})} | custom-call | flops 1048576 | bytes 65536 | tf_op jit(solution)/shard_map/final/pallas_call | solution.py:237
Async XLA Ops:
  0.0 34.7 %collective-permute-start.2 = (bf16[1024,1024]{1,0:T(8,128)(2,1)}, bf16[1024,1024]{1,0:T(8,128)(2,1)S(1)}, u32[]{:S(2)}, u32[]{:S(2)}) collective-permute-start(bf16[1024,1024]{1,0:T(8,128)(2,1)} %refs_2_.1), channel_id=1, source_target_pairs={{0,4},{2,6},{4,0},{5,13},{6,2},{7,15},{8,12},{9,1},{10,14},{11,3},... | collective-permute-start | bytes 6291464 | tf_op jit(solution)/shard_map/ppermute | solution.py:267
  4.8 35.8 %collective-permute-start.3 = (bf16[1024,1024]{1,0:T(8,128)(2,1)}, bf16[1024,1024]{1,0:T(8,128)(2,1)}, u32[]{:S(2)}, u32[]{:S(2)}) collective-permute-start(bf16[1024,1024]{1,0:T(8,128)(2,1)} %refs_2_.1), channel_id=1, source_target_pairs={{1,9},{3,11},{9,17},{11,19},{13,5},{15,7},{17,25},{19,27},{21,13},... | collective-permute-start | bytes 6291464 | tf_op jit(solution)/shard_map/ppermute | solution.py:267
  6.8 11.3 %collective-permute-start = (bf16[1024,128]{1,0:T(8,128)(2,1)}, bf16[1024,128]{1,0:T(8,128)(2,1)S(1)}, u32[]{:S(2)}, u32[]{:S(2)}) collective-permute-start(bf16[1024,128]{1,0:T(8,128)(2,1)} %query_ref.3), channel_id=1, source_target_pairs={{1,5},{3,7},{4,12},{5,1},{6,14},{7,3},{8,0},{9,13},{10,2},{11,15},... | collective-permute-start | bytes 786440 | tf_op jit(solution)/shard_map/ppermute | solution.py:267
  18.2 10.6 %collective-permute-start.1 = (bf16[1024,128]{1,0:T(8,128)(2,1)S(1)}, bf16[1024,128]{1,0:T(8,128)(2,1)S(1)}, u32[]{:S(2)}, u32[]{:S(2)}) collective-permute-start(bf16[1024,128]{1,0:T(8,128)(2,1)S(1)} %all_gather.3.refs_0_), channel_id=1, source_target_pairs={{1,4},{3,6},{4,13},{5,0},{6,15},{7,2},{8,1},{9,12},{10,3},{11,14},... | collective-permute-start | bytes 786440 | tf_op jit(solution)/shard_map/ppermute | solution.py:267
  19.6 0.7 %copy-start.1 = (s32[8,5]{1,0:T(8,128)S(1)}, s32[8,5]{1,0:T(8,128)}, u32[]{:S(2)}) copy-start(s32[8,5]{1,0:T(8,128)} %pattern_ref.1) | copy-start | bytes 484
  25.5 5.3 %copy-start.2 = (bf16[1024,1024]{1,0:T(8,128)(2,1)S(1)}, bf16[1024,1024]{1,0:T(8,128)(2,1)}, u32[]{:S(2)}) copy-start(bf16[1024,1024]{1,0:T(8,128)(2,1)} %refs_2_.1) | copy-start | bytes 6291460
  30.8 27.9 %collective-permute-start.6 = (bf16[1024,1024]{1,0:T(8,128)(2,1)S(1)}, bf16[1024,1024]{1,0:T(8,128)(2,1)S(1)}, u32[]{:S(2)}, u32[]{:S(2)}) collective-permute-start(bf16[1024,1024]{1,0:T(8,128)(2,1)S(1)} %copy-done.2), channel_id=1, source_target_pairs={{4,12},{6,14},{8,0},{10,2},{12,20},{14,22},{16,8},{18,10},{20,28},... | collective-permute-start | bytes 6291464 | tf_op jit(solution)/shard_map/ppermute | solution.py:267
  32.1 8.6 %collective-permute-start.4 = (bf16[1024,128]{1,0:T(8,128)(2,1)S(1)}, bf16[1024,128]{1,0:T(8,128)(2,1)S(1)}, u32[]{:S(2)}, u32[]{:S(2)}) collective-permute-start(bf16[1024,128]{1,0:T(8,128)(2,1)S(1)} %all_gather.3.refs_0_), channel_id=1, source_target_pairs={{1,9},{3,11},{9,17},{11,19},{13,5},{15,7},{17,25},{19,27},{21,13},... | collective-permute-start | bytes 786440 | tf_op jit(solution)/shard_map/ppermute | solution.py:267
  36.4 11.0 %copy-start = (bf16[1024,128]{1,0:T(8,128)(2,1)S(1)}, bf16[1024,128]{1,0:T(8,128)(2,1)}, u32[]{:S(2)}) copy-start(bf16[1024,128]{1,0:T(8,128)(2,1)} %query_ref.3) | copy-start | bytes 786436
  36.4 25.7 %collective-permute-start.8 = (bf16[1024,512]{1,0:T(8,128)(2,1)S(1)}, bf16[1024,512]{1,0:T(8,128)(2,1)S(1)}, u32[]{:S(2)}, u32[]{:S(2)}) collective-permute-start(bf16[1024,512]{1,0:T(8,128)(2,1)S(1)} %scores.2), channel_id=1, source_target_pairs={{0,8},{1,5},{2,10},{3,7},{5,1},{7,3},{8,16},{9,13},{10,18},{11,15}... | collective-permute-start | bytes 3145736 | tf_op jit(solution)/shard_map/ppermute | solution.py:267
  42.4 21.7 %collective-permute-start.7 = (bf16[1024,512]{1,0:T(8,128)(2,1)S(1)}, bf16[1024,512]{1,0:T(8,128)(2,1)S(1)}, u32[]{:S(2)}, u32[]{:S(2)}) collective-permute-start(bf16[1024,512]{1,0:T(8,128)(2,1)S(1)} %scores.3), channel_id=1, source_target_pairs={{0,8},{1,5},{2,10},{3,7},{5,1},{7,3},{8,16},{9,13},{10,18},{11,15}... | collective-permute-start | bytes 3145736 | tf_op jit(solution)/shard_map/ppermute | solution.py:267
  45.9 9.4 %collective-permute-start.5 = (bf16[1024,128]{1,0:T(8,128)(2,1)S(1)}, bf16[1024,128]{1,0:T(8,128)(2,1)S(1)}, u32[]{:S(2)}, u32[]{:S(2)}) collective-permute-start(bf16[1024,128]{1,0:T(8,128)(2,1)S(1)} %collective-permute-done.1.refs_0_.refs_1_), channel_id=1, source_target_pairs={{1,0},{3,2},{5,4},{7,6},{9,8},{11,10},{13,12},{15,14},{17,16},{19,... | collective-permute-start | bytes 786440 | tf_op jit(solution)/shard_map/ppermute | solution.py:267
where the time goes:
time: 65.6 us; the launch traced here: 65.2 us
  Pallas kernels  26.4 us (40%)
  starting transfers between devices  20.5 us (31%)
  waiting for transfers between devices  10.1 us (15%)
  blocking collectives  7.26 us (11%)
  local copies, waits for them, and re-layouts  0.7 us (1%)
    ppermute x9, starting transfers between devices, send(): return lax.ppermute(block, ('pb', 'ao'), route)  20.5 us
    pallas_call x4, Pallas kernels, kern_blocks(): pl.pallas_call(functools.partial(kern_kernel, RADIUS_FACTOR * math.sqrt(f...  16.6 us
    ppermute x9, waiting for transfers between devices, send(): return lax.ppermute(block, ('pb', 'ao'), route)  10.1 us
    all_gather x1, blocking collectives, per_device(): centre_own = lax.all_gather(centres, 'ao', axis=0, tiled=True)  7.26 us
    pallas_call x2, Pallas kernels, scores(): pl.pallas_call(functools.partial(score_kernel, terms, len(kerns), len(add...  3.51 us
    pallas_call x1, Pallas kernels, far_sum(): pl.pallas_call(functools.partial(far_kernel, min(256, rows)), in_specs=[S...  3.45 us
    pallas_call x2, Pallas kernels, final(): pl.pallas_call(functools.partial(final_kernel, scale, tile, half * width)...  2.23 us
  transfers between devices with their start and end apart: 9, of which 5 were waited for; matrix products, arithmetic and copies ran while one was open for 0% of the time, Pallas kernels for 39%

commit v1 on v0

--- a/solution.py
+++ b/solution.py
@@ -170,9 +170,8 @@
     out_ref = refs[-1]
     coefs = refs[kerns : len(refs) - 1 - adds]
 
-    @pl.loop(0, out_ref.shape[0] // tile)
-    def _(row):
-        rows = pl.ds(pl.multiple_of(row * tile, tile), tile)
+    for row in range(out_ref.shape[0] // tile):
+        rows = pl.ds(row * tile, tile)
         total = score_sum(terms, refs[:kerns], coefs, rows)
         if adds:
             total = total + refs[-2][rows, pl.ds(column, total.shape[1])].astype(F32)
@@ -183,7 +182,7 @@
     rows, width = kerns[0].shape[0], terms[0][4]
     adds = [] if add is None else [add]
     return pl.pallas_call(
-        functools.partial(score_kernel, terms, len(kerns), len(adds), column, min(256, rows)),
+        functools.partial(score_kernel, terms, len(kerns), len(adds), column, min(512, rows)),
         in_specs=[WHOLE] * (len(kerns) + len(coefs) + len(adds)),
         out_specs=WHOLE,
         out_shape=pltpu.VMEM((rows, width), dtype),
@@ -193,13 +192,27 @@
     )(*in_vmem(*kerns, *coefs, *adds))
 
 
-def far_kernel(tile, place_ref, kern_ref, far_0_ref, far_1_ref, add_ref, out_ref):
+def far_kernel(
+    scale, place_ref, kern_ref, far_0_ref, far_1_ref, add_ref, part_ref, out_ref, rest_ref, low_ref, sems
+):
+    width = part_ref.shape[1]
+    tile = min(512, kern_ref.shape[0])
+    tiles = [pl.ds(row * tile, tile) for row in range(kern_ref.shape[0] // tile)]
+    low, high = pl.ds(0, width), pl.ds(width, width)
+
     def sums(coef_ref):
-        @pl.loop(0, out_ref.shape[0] // tile)
-        def _(row):
-            rows = pl.ds(pl.multiple_of(row * tile, tile), tile)
-            total = jnp.dot(kern_ref[rows, :], coef_ref[...], preferred_element_type=F32)
-            out_ref[rows, :] = total + add_ref[rows, :]
+        copies = []
+        for k, rows in enumerate(tiles):
+            total = jnp.dot(kern_ref[rows, :], coef_ref[:, low], preferred_element_type=F32)
+            total = total + add_ref[rows, low] + part_ref[rows, :].astype(F32)
+            low_ref[rows, :] = (total * scale).astype(low_ref.dtype)
+            copies.append(pltpu.make_async_copy(low_ref.at[rows, :], out_ref.at[rows, low], sems.at[k]))
+            copies[k].start()
+        for rows in tiles:
+            total = jnp.dot(kern_ref[rows, :], coef_ref[:, high], preferred_element_type=F32)
+            rest_ref[rows, :] = total + add_ref[rows, high]
+        for copy in copies:
+            copy.wait()
 
     @pl.when(place_ref[1] == 0)
     def _():
@@ -210,41 +223,43 @@
         sums(far_1_ref)
 
 
-def far_sum(place, kern, far_0, far_1, add):
-    rows = kern.shape[0]
+def far_sum(place, kern, far_0, far_1, add, part, scale):
+    rows, width = part.shape
     return pl.pallas_call(
-        functools.partial(far_kernel, min(256, rows)),
-        in_specs=[SMEM] + [WHOLE] * 4,
-        out_specs=WHOLE,
-        out_shape=pltpu.VMEM(add.shape, add.dtype),
-        input_output_aliases={4: 0},
+        functools.partial(far_kernel, scale),
+        in_specs=[SMEM] + [WHOLE] * 5,
+        out_specs=[ANY, WHOLE],
+        out_shape=[jax.ShapeDtypeStruct(add.shape, BF16), pltpu.VMEM((rows, width), F32)],
+        scratch_shapes=[
+            pltpu.VMEM((rows, width), BF16),
+            pltpu.SemaphoreType.DMA((rows // min(512, rows),)),
+        ],
         compiler_params=pltpu.CompilerParams(vmem_limit_bytes=VMEM_LIMIT),
         cost_estimate=COST,
         name="far",
-    )(place, *in_vmem(kern, far_0, far_1, add))
-
-
-def final_kernel(scale, tile, column, add_ref, part_ref, *refs):
-    out_ref = refs[-1]
+    )(place, *in_vmem(kern, far_0, far_1, add, part))
+
+
+def final_kernel(scale, tile, add_ref, part_ref, _, out_ref):
     rows = pl.ds(pl.multiple_of(pl.program_id(0) * tile, tile), tile)
-    total = part_ref[rows, :].astype(F32) + add_ref[rows, pl.ds(column, out_ref.shape[1])]
+    total = part_ref[rows, :].astype(F32) + add_ref[rows, :]
     out_ref[...] = (total * scale).astype(out_ref.dtype)
 
 
-def final(add, part, scale, half, halves, out):
+def final(add, part, scale, out):
     rows, width = part.shape
     tile = min(512, rows)
     return pl.pallas_call(
-        functools.partial(final_kernel, scale, tile, half * width),
+        functools.partial(final_kernel, scale, tile),
         grid=(rows // tile,),
-        in_specs=[WHOLE] * 2 + ([] if out is None else [ANY]),
-        out_specs=pl.BlockSpec((tile, width), lambda r: (r, half)),
-        out_shape=jax.ShapeDtypeStruct((rows, width * halves), BF16),
-        input_output_aliases={} if out is None else {2: 0},
+        in_specs=[WHOLE, WHOLE, ANY],
+        out_specs=pl.BlockSpec((tile, width), lambda r: (r, 1)),
+        out_shape=jax.ShapeDtypeStruct(out.shape, out.dtype),
+        input_output_aliases={2: 0},
         compiler_params=pltpu.CompilerParams(vmem_limit_bytes=VMEM_LIMIT),
         cost_estimate=COST,
         name="final",
-    )(*in_vmem(add, part), *([] if out is None else [out]))
+    )(*in_vmem(add, part), out)
 
 
 def after(array, *others):
@@ -304,13 +319,9 @@
         (total[1],), queries, at_me, [[centre_own], [centre_near]], [at_me, at_near], [coefs_hbm, near], F32, [far_1]
     )
     kern_far = kern((own,), queries, at_me, [[centre_far_0, centre_far_1]], [at_far])
-    own = far_sum(place, kern_far, far_0, far_1, own)
-
     scale = 4.0 / radius**5
-    out = None
-    for h in range(2):
-        out = final(own, part[h], scale, h, 2, out)
-    return out
+    out, rest = far_sum(place, kern_far, far_0, far_1, own, part[0], scale)
+    return final(rest, part[1], scale, out)
 
 
 def solution(mesh):

time: 65.6 us -> 65.1 us (level)
  Pallas kernels: 26.4 us -> 23.9 us
  waiting for transfers between devices: 10.1 us -> 12.1 us
    ppermute x9, waiting for transfers between devices: 10.1 us -> 12.1 us  [send(): return lax.ppermute(block, ('pb', 'ao'), route)]
    pallas_call x3 -> x2, Pallas kernels: 5.68 us -> 4.17 us  [the longest x1 3.07 us: far_sum(): pl.pallas_call(functools.partial(far_kernel, scale), in_specs=[SMEM] + [W...]
    pallas_call x2, Pallas kernels: 3.51 us -> 2.5 us  [scores(): pl.pallas_call(functools.partial(score_kernel, terms, len(kerns), len(add...]
  transfers between devices with their start and end apart: 9 -> 9, of which waited for: 5 -> 5; matrix products, arithmetic and copies ran while one was open for 0% -> 0% of each run, Pallas kernels for 39% -> 35%
where the time goes in v1:
time: 65.1 us; the launch traced here: 64.7 us
  Pallas kernels  23.9 us (37%)
  starting transfers between devices  20.5 us (31%)
  waiting for transfers between devices  12.1 us (19%)
  blocking collectives  7.26 us (11%)
  local copies, waits for them, and re-layouts  0.7 us (1%)
    ppermute x9, starting transfers between devices, send(): return lax.ppermute(block, ('pb', 'ao'), route)  20.5 us
    pallas_call x4, Pallas kernels, kern_blocks(): pl.pallas_call(functools.partial(kern_kernel, RADIUS_FACTOR * math.sqrt(f...  16.6 us
    ppermute x9, waiting for transfers between devices, send(): return lax.ppermute(block, ('pb', 'ao'), route)  12.1 us
    all_gather x1, blocking collectives, per_device(): centre_own = lax.all_gather(centres, 'ao', axis=0, tiled=True)  7.26 us
    pallas_call x1, Pallas kernels, far_sum(): pl.pallas_call(functools.partial(far_kernel, scale), in_specs=[SMEM] + [W...  3.07 us
    pallas_call x2, Pallas kernels, scores(): pl.pallas_call(functools.partial(score_kernel, terms, len(kerns), len(add...  2.5 us
  transfers between devices with their start and end apart: 9, of which 5 were waited for; matrix products, arithmetic and copies ran while one was open for 0% of the time, Pallas kernels for 35%

profile of v1, /device:TPU:0, one launch (start us, length us, event | category | flops | bytes accessed | tf_op | source)
XLA Modules:
  0.0 64.7 jit_solution(16292251263818072657)
XLA Ops:
  0.0 4.8 %collective-permute-start.2 = (bf16[1024,1024]{1,0:T(8,128)(2,1)}, bf16[1024,1024]{1,0:T(8,128)(2,1)S(1)}, u32[]{:S(2)}, u32[]{:S(2)}) collective-permute-start(bf16[1024,1024]{1,0:T(8,128)(2,1)} %refs_2_.1), channel_id=1, source_target_pairs={{0,4},{2,6},{4,0},{5,13},{6,2},{7,15},{8,12},{9,1},{10,14},{11,3},... | collective-permute-start | bytes 6291464 | tf_op jit(solution)/shard_map/ppermute | solution.py:282
  4.8 2.0 %collective-permute-start.3 = (bf16[1024,1024]{1,0:T(8,128)(2,1)}, bf16[1024,1024]{1,0:T(8,128)(2,1)}, u32[]{:S(2)}, u32[]{:S(2)}) collective-permute-start(bf16[1024,1024]{1,0:T(8,128)(2,1)} %refs_2_.1), channel_id=1, source_target_pairs={{1,9},{3,11},{9,17},{11,19},{13,5},{15,7},{17,25},{19,27},{21,13},... | collective-permute-start | bytes 6291464 | tf_op jit(solution)/shard_map/ppermute | solution.py:282
  6.8 1.3 %collective-permute-start = (bf16[1024,128]{1,0:T(8,128)(2,1)}, bf16[1024,128]{1,0:T(8,128)(2,1)S(1)}, u32[]{:S(2)}, u32[]{:S(2)}) collective-permute-start(bf16[1024,128]{1,0:T(8,128)(2,1)} %query_ref.3), channel_id=1, source_target_pairs={{1,5},{3,7},{4,12},{5,1},{6,14},{7,3},{8,0},{9,13},{10,2},{11,15},... | collective-permute-start | bytes 786440 | tf_op jit(solution)/shard_map/ppermute | solution.py:282
  8.1 7.3 %all_gather.3.refs_0_ = bf16[1024,128]{1,0:T(8,128)(2,1)S(1)} all-gather(bf16[256,128]{1,0:T(8,128)(2,1)} %param.5), channel_id=1, replica_groups=mesh['pb'=8,'ao'=4] {'ao'}, dimensions={0}, use_global_device_ids=true | all-gather | bytes 327680 | tf_op jit(solution)/shard_map/all_gather | solution.py:293
  15.4 2.8 %collective-permute-done.query_ref = bf16[1024,128]{1,0:T(8,128)(2,1)S(1)} collective-permute-done((bf16[1024,128]{1,0:T(8,128)(2,1)}, bf16[1024,128]{1,0:T(8,128)(2,1)S(1)}, u32[]{:S(2)}, u32[]{:S(2)}) %collective-permute-start) | collective-permute-done | bytes 262176 | tf_op jit(solution)/shard_map/ppermute | solution.py:282
  18.2 1.3 %collective-permute-start.1 = (bf16[1024,128]{1,0:T(8,128)(2,1)S(1)}, bf16[1024,128]{1,0:T(8,128)(2,1)S(1)}, u32[]{:S(2)}, u32[]{:S(2)}) collective-permute-start(bf16[1024,128]{1,0:T(8,128)(2,1)S(1)} %all_gather.3.refs_0_), channel_id=1, source_target_pairs={{1,4},{3,6},{4,13},{5,0},{6,15},{7,2},{8,1},{9,12},{10,3},{11,14},... | collective-permute-start | bytes 786440 | tf_op jit(solution)/shard_map/ppermute | solution.py:282
  19.5 0.1 pad_add_fusion.place_ref
  19.5 0.0 copy-start.1
  19.6 0.7 %copy-done.1 = s32[8,5]{1,0:T(8,128)S(1)} copy-done((s32[8,5]{1,0:T(8,128)S(1)}, s32[8,5]{1,0:T(8,128)}, u32[]{:S(2)}) %copy-start.1) | copy-done | bytes 184
  20.2 0.6 cuts.1.cut_ref
  20.9 4.5 %kern.4.refs_2_ = bf16[1024,1024]{1,0:T(8,128)(2,1)S(1)} custom-call(f32[5,8,256]{2,1,0:T(8,128)S(1)} %cuts.1.cut_ref, bf16[1024,128]{1,0:T(8,128)(2,1)S(1)} %collective-permute-done.query_ref, bf16[1024,128]{1,0:T(8,128)(2,1)S(1)} %all_gather.3.refs_0_, bf16[1024,1024]{1,0:T(8,128)(2,1)} %refs_2_.1), custom_call_target="tpu_custom_call" | custom-call | flops 1048576 | bytes 65536 | tf_op jit(solution)/shard_map/kern/pallas_call | solution.py:141
  25.4 0.0 copy-start.2
  25.5 3.3 %collective-permute-done.1.refs_0_.refs_1_ = bf16[1024,128]{1,0:T(8,128)(2,1)S(1)} collective-permute-done((bf16[1024,128]{1,0:T(8,128)(2,1)S(1)}, bf16[1024,128]{1,0:T(8,128)(2,1)S(1)}, u32[]{:S(2)}, u32[]{:S(2)}) %collective-permute-start.1) | collective-permute-done | bytes 262176 | tf_op jit(solution)/shard_map/ppermute | solution.py:282
  28.7 2.0 %kern.5.refs_0_ = bf16[1024,1024]{1,0:T(8,128)(2,1)S(1)} custom-call(f32[5,8,256]{2,1,0:T(8,128)S(1)} %cuts.1.cut_ref, bf16[1024,128]{1,0:T(8,128)(2,1)S(1)} %collective-permute-done.query_ref, bf16[1024,128]{1,0:T(8,128)(2,1)S(1)} %collective-permute-done.1.refs_0_.refs_1_), custom_call_target="tpu_custom_call" | custom-call | flops 1048576 | bytes 65536 | tf_op jit(solution)/shard_map/kern/pallas_call | solution.py:141
  30.8 0.0 copy-done.2
  30.8 1.3 %collective-permute-start.6 = (bf16[1024,1024]{1,0:T(8,128)(2,1)S(1)}, bf16[1024,1024]{1,0:T(8,128)(2,1)S(1)}, u32[]{:S(2)}, u32[]{:S(2)}) collective-permute-start(bf16[1024,1024]{1,0:T(8,128)(2,1)S(1)} %copy-done.2), channel_id=1, source_target_pairs={{4,12},{6,14},{8,0},{10,2},{12,20},{14,22},{16,8},{18,10},{20,28},... | collective-permute-start | bytes 6291464 | tf_op jit(solution)/shard_map/ppermute | solution.py:282
  32.1 0.7 %collective-permute-start.4 = (bf16[1024,128]{1,0:T(8,128)(2,1)S(1)}, bf16[1024,128]{1,0:T(8,128)(2,1)S(1)}, u32[]{:S(2)}, u32[]{:S(2)}) collective-permute-start(bf16[1024,128]{1,0:T(8,128)(2,1)S(1)} %all_gather.3.refs_0_), channel_id=1, source_target_pairs={{1,9},{3,11},{9,17},{11,19},{13,5},{15,7},{17,25},{19,27},{21,13},... | collective-permute-start | bytes 786440 | tf_op jit(solution)/shard_map/ppermute | solution.py:282
  32.8 1.9 %collective-permute-done.2.refs_1_.refs_3_ = bf16[1024,1024]{1,0:T(8,128)(2,1)S(1)} collective-permute-done((bf16[1024,1024]{1,0:T(8,128)(2,1)}, bf16[1024,1024]{1,0:T(8,128)(2,1)S(1)}, u32[]{:S(2)}, u32[]{:S(2)}) %collective-permute-start.2) | collective-permute-done | bytes 2097184 | tf_op jit(solution)/shard_map/ppermute | solution.py:282
  34.7 1.3 %scores.2 = bf16[1024,512]{1,0:T(8,128)(2,1)S(1)} custom-call(bf16[1024,1024]{1,0:T(8,128)(2,1)S(1)} %kern.5.refs_0_, bf16[1024,1024]{1,0:T(8,128)(2,1)S(1)} %collective-permute-done.2.refs_1_.refs_3_, bf16[1024,1024]{1,0:T(8,128)(2,1)S(1)} %kern.4.refs_2_), custom_call_target="tpu_custom_call" | custom-call | flops 1048576 | bytes 65536 | tf_op jit(solution)/shard_map/scores/pallas_call | solution.py:184
  35.9 0.0 copy-start
  35.9 4.2 %collective-permute-start.7 = (bf16[1024,512]{1,0:T(8,128)(2,1)S(1)}, bf16[1024,512]{1,0:T(8,128)(2,1)S(1)}, u32[]{:S(2)}, u32[]{:S(2)}) collective-permute-start(bf16[1024,512]{1,0:T(8,128)(2,1)S(1)} %scores.2), channel_id=1, source_target_pairs={{0,8},{1,5},{2,10},{3,7},{5,1},{7,3},{8,16},{9,13},{10,18},{11,15}... | collective-permute-start | bytes 3145736 | tf_op jit(solution)/shard_map/ppermute | solution.py:282
  40.2 0.0 collective-permute-done.4.refs_1_
  40.2 0.0 collective-permute-done.3.refs_4_
  40.2 1.3 %scores.3 = bf16[1024,512]{1,0:T(8,128)(2,1)S(1)} custom-call(bf16[1024,1024]{1,0:T(8,128)(2,1)S(1)} %kern.5.refs_0_, bf16[1024,1024]{1,0:T(8,128)(2,1)S(1)} %collective-permute-done.2.refs_1_.refs_3_, bf16[1024,1024]{1,0:T(8,128)(2,1)S(1)} %kern.4.refs_2_), custom_call_target="tpu_custom_call" | custom-call | flops 1048576 | bytes 65536 | tf_op jit(solution)/shard_map/scores/pallas_call | solution.py:184
  41.4 3.5 %collective-permute-start.8 = (bf16[1024,512]{1,0:T(8,128)(2,1)S(1)}, bf16[1024,512]{1,0:T(8,128)(2,1)S(1)}, u32[]{:S(2)}, u32[]{:S(2)}) collective-permute-start(bf16[1024,512]{1,0:T(8,128)(2,1)S(1)} %scores.3), channel_id=1, source_target_pairs={{0,8},{1,5},{2,10},{3,7},{5,1},{7,3},{8,16},{9,13},{10,18},{11,15}... | collective-permute-start | bytes 3145736 | tf_op jit(solution)/shard_map/ppermute | solution.py:282
  44.9 1.5 %collective-permute-start.5 = (bf16[1024,128]{1,0:T(8,128)(2,1)S(1)}, bf16[1024,128]{1,0:T(8,128)(2,1)S(1)}, u32[]{:S(2)}, u32[]{:S(2)}) collective-permute-start(bf16[1024,128]{1,0:T(8,128)(2,1)S(1)} %collective-permute-done.1.refs_0_.refs_1_), channel_id=1, source_target_pairs={{1,0},{3,2},{5,4},{7,6},{9,8},{11,10},{13,12},{15,14},{17,16},{19,... | collective-permute-start | bytes 786440 | tf_op jit(solution)/shard_map/ppermute | solution.py:282
  46.4 0.0 copy-done
  46.4 7.9 %kern.6 = (f32[1024,1024]{1,0:T(8,128)S(1)}, bf16[1024,1024]{1,0:T(8,128)(2,1)S(1)}) custom-call(f32[5,8,256]{2,1,0:T(8,128)S(1)} %cuts.1.cut_ref, bf16[1024,128]{1,0:T(8,128)(2,1)S(1)} %copy-done, bf16[1024,128]{1,0:T(8,128)(2,1)S(1)} %all_gather.3.refs_0_, bf16[1024,128]{1,0:T(8,128)(2,1)S(1)} %collective-permute-done.1.refs_0_.refs_1_, ...), custom_call_target="tpu_custom_call" | custom-call | flops 1048576 | bytes 65536 | tf_op jit(solution)/shard_map/kern/pallas_call | solution.py:141
  54.3 0.0 collective-permute-done.5.refs_0_
  54.3 2.1 %kern.7.kern_ref = bf16[1024,1024]{1,0:T(8,128)(2,1)S(1)} custom-call(f32[5,8,256]{2,1,0:T(8,128)S(1)} %cuts.1.cut_ref, bf16[1024,128]{1,0:T(8,128)(2,1)S(1)} %copy-done, bf16[1024,128]{1,0:T(8,128)(2,1)S(1)} %collective-permute-done.5.refs_0_, bf16[1024,128]{1,0:T(8,128)(2,1)S(1)} %collective-permute-done.4.refs_1_), custom_call_target="tpu_custom_call" | custom-call | flops 1048576 | bytes 65536 | tf_op jit(solution)/shard_map/kern/pallas_call | solution.py:141
  56.4 2.3 %collective-permute-done.6.far_0_ref = bf16[1024,1024]{1,0:T(8,128)(2,1)S(1)} collective-permute-done((bf16[1024,1024]{1,0:T(8,128)(2,1)S(1)}, bf16[1024,1024]{1,0:T(8,128)(2,1)S(1)}, u32[]{:S(2)}, u32[]{:S(2)}) %collective-permute-start.6) | collective-permute-done | bytes 2097184 | tf_op jit(solution)/shard_map/ppermute | solution.py:282
  58.7 0.0 collective-permute-done.7.part_ref
  58.7 3.1 %far.1 = (bf16[1024,1024]{1,0:T(8,128)(2,1)}, f32[1024,512]{1,0:T(8,128)S(1)}) custom-call(s32[2]{0:T(128)S(1)} %pad_add_fusion.place_ref, bf16[1024,1024]{1,0:T(8,128)(2,1)S(1)} %kern.7.kern_ref, bf16[1024,1024]{1,0:T(8,128)(2,1)S(1)} %collective-permute-done.6.far_0_ref, bf16[1024,1024]{1,0:T(8,128)(2,1)S(1)} %get-tuple-element.28.far_1_ref, ...), custom_call_target="tpu_custom_call" | custom-call | flops 1048576 | bytes 65536 | tf_op jit(solution)/shard_map/far/pallas_call | solution.py:228
  61.8 1.8 %collective-permute-done.8.part_ref = bf16[1024,512]{1,0:T(8,128)(2,1)S(1)} collective-permute-done((bf16[1024,512]{1,0:T(8,128)(2,1)S(1)}, bf16[1024,512]{1,0:T(8,128)(2,1)S(1)}, u32[]{:S(2)}, u32[]{:S(2)}) %collective-permute-start.8) | collective-permute-done | bytes 1048608 | tf_op jit(solution)/shard_map/ppermute | solution.py:282
  63.6 1.1 %final.1 = bf16[1024,1024]{1,0:T(8,128)(2,1)} custom-call(f32[1024,512]{1,0:T(8,128)S(1)} %get-tuple-element.29.add_ref, bf16[1024,512]{1,0:T(8,128)(2,1)S(1)} %collective-permute-done.8.part_ref, bf16[1024,1024]{1,0:T(8,128)(2,1)} %get-tuple-element.30._), custom_call_target="tpu_custom_call", output_to_operand_aliasing={{}: (2, {})} | custom-call | flops 1048576 | bytes 65536 | tf_op jit(solution)/shard_map/final/pallas_call | solution.py:252
Async XLA Ops:
  0.0 34.7 %collective-permute-start.2 = (bf16[1024,1024]{1,0:T(8,128)(2,1)}, bf16[1024,1024]{1,0:T(8,128)(2,1)S(1)}, u32[]{:S(2)}, u32[]{:S(2)}) collective-permute-start(bf16[1024,1024]{1,0:T(8,128)(2,1)} %refs_2_.1), channel_id=1, source_target_pairs={{0,4},{2,6},{4,0},{5,13},{6,2},{7,15},{8,12},{9,1},{10,14},{11,3},... | collective-permute-start | bytes 6291464 | tf_op jit(solution)/shard_map/ppermute | solution.py:282
  4.8 35.3 %collective-permute-start.3 = (bf16[1024,1024]{1,0:T(8,128)(2,1)}, bf16[1024,1024]{1,0:T(8,128)(2,1)}, u32[]{:S(2)}, u32[]{:S(2)}) collective-permute-start(bf16[1024,1024]{1,0:T(8,128)(2,1)} %refs_2_.1), channel_id=1, source_target_pairs={{1,9},{3,11},{9,17},{11,19},{13,5},{15,7},{17,25},{19,27},{21,13},... | collective-permute-start | bytes 6291464 | tf_op jit(solution)/shard_map/ppermute | solution.py:282
  6.8 11.3 %collective-permute-start = (bf16[1024,128]{1,0:T(8,128)(2,1)}, bf16[1024,128]{1,0:T(8,128)(2,1)S(1)}, u32[]{:S(2)}, u32[]{:S(2)}) collective-permute-start(bf16[1024,128]{1,0:T(8,128)(2,1)} %query_ref.3), channel_id=1, source_target_pairs={{1,5},{3,7},{4,12},{5,1},{6,14},{7,3},{8,0},{9,13},{10,2},{11,15},... | collective-permute-start | bytes 786440 | tf_op jit(solution)/shard_map/ppermute | solution.py:282
  18.2 10.6 %collective-permute-start.1 = (bf16[1024,128]{1,0:T(8,128)(2,1)S(1)}, bf16[1024,128]{1,0:T(8,128)(2,1)S(1)}, u32[]{:S(2)}, u32[]{:S(2)}) collective-permute-start(bf16[1024,128]{1,0:T(8,128)(2,1)S(1)} %all_gather.3.refs_0_), channel_id=1, source_target_pairs={{1,4},{3,6},{4,13},{5,0},{6,15},{7,2},{8,1},{9,12},{10,3},{11,14},... | collective-permute-start | bytes 786440 | tf_op jit(solution)/shard_map/ppermute | solution.py:282
  19.5 0.7 %copy-start.1 = (s32[8,5]{1,0:T(8,128)S(1)}, s32[8,5]{1,0:T(8,128)}, u32[]{:S(2)}) copy-start(s32[8,5]{1,0:T(8,128)} %pattern_ref.1) | copy-start | bytes 484
  25.4 5.3 %copy-start.2 = (bf16[1024,1024]{1,0:T(8,128)(2,1)S(1)}, bf16[1024,1024]{1,0:T(8,128)(2,1)}, u32[]{:S(2)}) copy-start(bf16[1024,1024]{1,0:T(8,128)(2,1)} %refs_2_.1) | copy-start | bytes 6291460
  30.8 27.9 %collective-permute-start.6 = (bf16[1024,1024]{1,0:T(8,128)(2,1)S(1)}, bf16[1024,1024]{1,0:T(8,128)(2,1)S(1)}, u32[]{:S(2)}, u32[]{:S(2)}) collective-permute-start(bf16[1024,1024]{1,0:T(8,128)(2,1)S(1)} %copy-done.2), channel_id=1, source_target_pairs={{4,12},{6,14},{8,0},{10,2},{12,20},{14,22},{16,8},{18,10},{20,28},... | collective-permute-start | bytes 6291464 | tf_op jit(solution)/shard_map/ppermute | solution.py:282
  32.1 8.1 %collective-permute-start.4 = (bf16[1024,128]{1,0:T(8,128)(2,1)S(1)}, bf16[1024,128]{1,0:T(8,128)(2,1)S(1)}, u32[]{:S(2)}, u32[]{:S(2)}) collective-permute-start(bf16[1024,128]{1,0:T(8,128)(2,1)S(1)} %all_gather.3.refs_0_), channel_id=1, source_target_pairs={{1,9},{3,11},{9,17},{11,19},{13,5},{15,7},{17,25},{19,27},{21,13},... | collective-permute-start | bytes 786440 | tf_op jit(solution)/shard_map/ppermute | solution.py:282
  35.9 10.5 %copy-start = (bf16[1024,128]{1,0:T(8,128)(2,1)S(1)}, bf16[1024,128]{1,0:T(8,128)(2,1)}, u32[]{:S(2)}) copy-start(bf16[1024,128]{1,0:T(8,128)(2,1)} %query_ref.3) | copy-start | bytes 786436
  35.9 22.8 %collective-permute-start.7 = (bf16[1024,512]{1,0:T(8,128)(2,1)S(1)}, bf16[1024,512]{1,0:T(8,128)(2,1)S(1)}, u32[]{:S(2)}, u32[]{:S(2)}) collective-permute-start(bf16[1024,512]{1,0:T(8,128)(2,1)S(1)} %scores.2), channel_id=1, source_target_pairs={{0,8},{1,5},{2,10},{3,7},{5,1},{7,3},{8,16},{9,13},{10,18},{11,15}... | collective-permute-start | bytes 3145736 | tf_op jit(solution)/shard_map/ppermute | solution.py:282
  41.4 22.2 %collective-permute-start.8 = (bf16[1024,512]{1,0:T(8,128)(2,1)S(1)}, bf16[1024,512]{1,0:T(8,128)(2,1)S(1)}, u32[]{:S(2)}, u32[]{:S(2)}) collective-permute-start(bf16[1024,512]{1,0:T(8,128)(2,1)S(1)} %scores.3), channel_id=1, source_target_pairs={{0,8},{1,5},{2,10},{3,7},{5,1},{7,3},{8,16},{9,13},{10,18},{11,15}... | collective-permute-start | bytes 3145736 | tf_op jit(solution)/shard_map/ppermute | solution.py:282
  44.9 9.4 %collective-permute-start.5 = (bf16[1024,128]{1,0:T(8,128)(2,1)S(1)}, bf16[1024,128]{1,0:T(8,128)(2,1)S(1)}, u32[]{:S(2)}, u32[]{:S(2)}) collective-permute-start(bf16[1024,128]{1,0:T(8,128)(2,1)S(1)} %collective-permute-done.1.refs_0_.refs_1_), channel_id=1, source_target_pairs={{1,0},{3,2},{5,4},{7,6},{9,8},{11,10},{13,12},{15,14},{17,16},{19,... | collective-permute-start | bytes 786440 | tf_op jit(solution)/shard_map/ppermute | solution.py:282

commit v2 on v1

--- a/solution.py
+++ b/solution.py
@@ -60,7 +60,7 @@
         functools.partial(cut_kernel, radius, pairs),
         in_specs=[SMEM, SMEM],
         out_specs=WHOLE,
-        out_shape=pltpu.VMEM((len(pairs), 8, 256), F32),
+        out_shape=pltpu.VMEM((len(pairs), 8, 512), F32),
         compiler_params=pltpu.CompilerParams(vmem_limit_bytes=VMEM_LIMIT),
         cost_estimate=COST,
         name="cuts",
@@ -69,7 +69,7 @@
 
 def kern_tile(query, centre_wide, cut_ref, radius, out_ref, column):
     depth = centre_wide.shape[0]
-    columns = min(256, depth)
+    columns = min(512, depth)
     for start in range(0, depth, columns):
         square = lax.dot_general(
             query, centre_wide[pl.ds(start, columns), :], (((1,), (1,)), ((), ())), preferred_element_type=F32
@@ -198,7 +198,7 @@
     width = part_ref.shape[1]
     tile = min(512, kern_ref.shape[0])
     tiles = [pl.ds(row * tile, tile) for row in range(kern_ref.shape[0] // tile)]
-    low, high = pl.ds(0, width), pl.ds(width, width)
+    low, high = pl.ds(0, width), pl.ds(width, add_ref.shape[1] - width)
 
     def sums(coef_ref):
         copies = []
@@ -229,7 +229,7 @@
         functools.partial(far_kernel, scale),
         in_specs=[SMEM] + [WHOLE] * 5,
         out_specs=[ANY, WHOLE],
-        out_shape=[jax.ShapeDtypeStruct(add.shape, BF16), pltpu.VMEM((rows, width), F32)],
+        out_shape=[jax.ShapeDtypeStruct(add.shape, BF16), pltpu.VMEM((rows, add.shape[1] - width), F32)],
         scratch_shapes=[
             pltpu.VMEM((rows, width), BF16),
             pltpu.SemaphoreType.DMA((rows // min(512, rows),)),
@@ -240,22 +240,33 @@
     )(place, *in_vmem(kern, far_0, far_1, add, part))
 
 
-def final_kernel(scale, tile, add_ref, part_ref, _, out_ref):
-    rows = pl.ds(pl.multiple_of(pl.program_id(0) * tile, tile), tile)
-    total = part_ref[rows, :].astype(F32) + add_ref[rows, :]
-    out_ref[...] = (total * scale).astype(out_ref.dtype)
+def final_kernel(scale, add_ref, part_ref, _, out_ref, last_ref, sems):
+    rows, width = part_ref.shape
+    tile = min(256, rows)
+    columns = pl.ds(out_ref.shape[1] - width, width)
+    copies = []
+    for k in range(rows // tile):
+        span = pl.ds(k * tile, tile)
+        total = part_ref[span, :].astype(F32) + add_ref[span, :]
+        last_ref[span, :] = (total * scale).astype(last_ref.dtype)
+        copies.append(pltpu.make_async_copy(last_ref.at[span, :], out_ref.at[span, columns], sems.at[k]))
+        copies[k].start()
+    for copy in copies:
+        copy.wait()
 
 
 def final(add, part, scale, out):
     rows, width = part.shape
-    tile = min(512, rows)
     return pl.pallas_call(
-        functools.partial(final_kernel, scale, tile),
-        grid=(rows // tile,),
+        functools.partial(final_kernel, scale),
         in_specs=[WHOLE, WHOLE, ANY],
-        out_specs=pl.BlockSpec((tile, width), lambda r: (r, 1)),
+        out_specs=ANY,
         out_shape=jax.ShapeDtypeStruct(out.shape, out.dtype),
         input_output_aliases={2: 0},
+        scratch_shapes=[
+            pltpu.VMEM((rows, width), BF16),
+            pltpu.SemaphoreType.DMA((rows // min(256, rows),)),
+        ],
         compiler_params=pltpu.CompilerParams(vmem_limit_bytes=VMEM_LIMIT),
         cost_estimate=COST,
         name="final",
@@ -301,7 +312,8 @@
         cuts = tuple(pairs.index((query_at, centre_at)) for centre_at in at)
         return kern_blocks(after(cut_rows, *order), queries, centres, cuts, *scored)
 
-    width = coefs.shape[1] // 2
+    whole = coefs.shape[1]
+    first = whole * 5 // 8 if whole % 1024 == 0 else whole // 2
     coefs_hbm = pltpu.with_memory_space_constraint(coefs, pltpu.HBM)
     base_t = kern((), query_t, at_target, [[centre_own]], [at_me], [coefs_hbm])
     centre_far_1 = send(after(centre_own, base_t), nobody, front(1))
@@ -309,10 +321,10 @@
     far_0 = send(after(coefs, kern_t), back(0), nobody)
     near = after(near, kern_t)
     total, part = [], []
-    for h in range(2):
+    for h, (column, width) in enumerate(((0, first), (first, whole - first))):
         if h == 1:
             near = after(near, total[0], far_1, centre_far_1)
-        total.append(scores([kern_t], [near], ((0, 0, 0, h * width, width),), BF16, base_t, h * width))
+        total.append(scores([kern_t], [near], ((0, 0, 0, column, width),), BF16, base_t, column))
         part.append(send(total[h], front(0), partner(1)))
     centre_far_0 = send(after(centre_near, total[1]), nobody, lambda i: (i, 0))
     own, far_1 = kern(

time: 65.1 us -> 69.2 us (1.063); the launches traced: 64.7 us -> 68.1 us
  waiting for transfers between devices: 12.1 us -> 14.2 us
  Pallas kernels: 23.9 us -> 25 us
    ppermute x9, waiting for transfers between devices: 12.1 us -> 14.2 us  [send(): return lax.ppermute(block, ('pb', 'ao'), route)]
    pallas_call x1, Pallas kernels: 3.07 us -> 3.84 us  [far_sum(): pl.pallas_call(functools.partial(far_kernel, scale), in_specs=[SMEM] + [W...]
where the time goes in v2:
time: 69.2 us; the launch traced here: 68.1 us
  Pallas kernels  25 us (36%)
  starting transfers between devices  20.5 us (30%)
  waiting for transfers between devices  14.2 us (21%)
  blocking collectives  7.26 us (10%)
  local copies, waits for them, and re-layouts  0.7 us (1%)
    ppermute x9, starting transfers between devices, send(): return lax.ppermute(block, ('pb', 'ao'), route)  20.5 us
    pallas_call x4, Pallas kernels, kern_blocks(): pl.pallas_call(functools.partial(kern_kernel, RADIUS_FACTOR * math.sqrt(f...  16.5 us
    ppermute x9, waiting for transfers between devices, send(): return lax.ppermute(block, ('pb', 'ao'), route)  14.2 us
    all_gather x1, blocking collectives, per_device(): centre_own = lax.all_gather(centres, 'ao', axis=0, tiled=True)  7.26 us
    pallas_call x1, Pallas kernels, far_sum(): pl.pallas_call(functools.partial(far_kernel, scale), in_specs=[SMEM] + [W...  3.84 us
    pallas_call x2, Pallas kernels, scores(): pl.pallas_call(functools.partial(score_kernel, terms, len(kerns), len(add...  3.04 us
  transfers between devices with their start and end apart: 9, of which 5 were waited for; matrix products, arithmetic and copies ran while one was open for 0% of the time, Pallas kernels for 35%

profile of v2, /device:TPU:0, one launch (start us, length us, event | category | flops | bytes accessed | tf_op | source)
XLA Modules:
  0.0 68.1 jit_solution(18248231300956876794)
XLA Ops:
  0.0 4.8 %collective-permute-start.2 = (bf16[1024,1024]{1,0:T(8,128)(2,1)}, bf16[1024,1024]{1,0:T(8,128)(2,1)S(1)}, u32[]{:S(2)}, u32[]{:S(2)}) collective-permute-start(bf16[1024,1024]{1,0:T(8,128)(2,1)} %refs_2_.1), channel_id=1, source_target_pairs={{0,4},{2,6},{4,0},{5,13},{6,2},{7,15},{8,12},{9,1},{10,14},{11,3},... | collective-permute-start | bytes 6291464 | tf_op jit(solution)/shard_map/ppermute | solution.py:293
  4.8 2.0 %collective-permute-start.3 = (bf16[1024,1024]{1,0:T(8,128)(2,1)}, bf16[1024,1024]{1,0:T(8,128)(2,1)}, u32[]{:S(2)}, u32[]{:S(2)}) collective-permute-start(bf16[1024,1024]{1,0:T(8,128)(2,1)} %refs_2_.1), channel_id=1, source_target_pairs={{1,9},{3,11},{9,17},{11,19},{13,5},{15,7},{17,25},{19,27},{21,13},... | collective-permute-start | bytes 6291464 | tf_op jit(solution)/shard_map/ppermute | solution.py:293
  6.8 1.3 %collective-permute-start = (bf16[1024,128]{1,0:T(8,128)(2,1)}, bf16[1024,128]{1,0:T(8,128)(2,1)S(1)}, u32[]{:S(2)}, u32[]{:S(2)}) collective-permute-start(bf16[1024,128]{1,0:T(8,128)(2,1)} %query_ref.3), channel_id=1, source_target_pairs={{1,5},{3,7},{4,12},{5,1},{6,14},{7,3},{8,0},{9,13},{10,2},{11,15},... | collective-permute-start | bytes 786440 | tf_op jit(solution)/shard_map/ppermute | solution.py:293
  8.1 7.3 %all_gather.3.refs_0_ = bf16[1024,128]{1,0:T(8,128)(2,1)S(1)} all-gather(bf16[256,128]{1,0:T(8,128)(2,1)} %param.5), channel_id=1, replica_groups=mesh['pb'=8,'ao'=4] {'ao'}, dimensions={0}, use_global_device_ids=true | all-gather | bytes 327680 | tf_op jit(solution)/shard_map/all_gather | solution.py:304
  15.4 2.8 %collective-permute-done.query_ref = bf16[1024,128]{1,0:T(8,128)(2,1)S(1)} collective-permute-done((bf16[1024,128]{1,0:T(8,128)(2,1)}, bf16[1024,128]{1,0:T(8,128)(2,1)S(1)}, u32[]{:S(2)}, u32[]{:S(2)}) %collective-permute-start) | collective-permute-done | bytes 262176 | tf_op jit(solution)/shard_map/ppermute | solution.py:293
  18.2 1.3 %collective-permute-start.1 = (bf16[1024,128]{1,0:T(8,128)(2,1)S(1)}, bf16[1024,128]{1,0:T(8,128)(2,1)S(1)}, u32[]{:S(2)}, u32[]{:S(2)}) collective-permute-start(bf16[1024,128]{1,0:T(8,128)(2,1)S(1)} %all_gather.3.refs_0_), channel_id=1, source_target_pairs={{1,4},{3,6},{4,13},{5,0},{6,15},{7,2},{8,1},{9,12},{10,3},{11,14},... | collective-permute-start | bytes 786440 | tf_op jit(solution)/shard_map/ppermute | solution.py:293
  19.5 0.1 pad_add_fusion.place_ref
  19.5 0.0 copy-start.1
  19.6 0.7 %copy-done.1 = s32[8,5]{1,0:T(8,128)S(1)} copy-done((s32[8,5]{1,0:T(8,128)S(1)}, s32[8,5]{1,0:T(8,128)}, u32[]{:S(2)}) %copy-start.1) | copy-done | bytes 184
  20.2 0.6 cuts.1.cut_ref
  20.9 4.5 %kern.4.refs_2_ = bf16[1024,1024]{1,0:T(8,128)(2,1)S(1)} custom-call(f32[5,8,512]{2,1,0:T(8,128)S(1)} %cuts.1.cut_ref, bf16[1024,128]{1,0:T(8,128)(2,1)S(1)} %collective-permute-done.query_ref, bf16[1024,128]{1,0:T(8,128)(2,1)S(1)} %all_gather.3.refs_0_, bf16[1024,1024]{1,0:T(8,128)(2,1)} %refs_2_.1), custom_call_target="tpu_custom_call" | custom-call | flops 1048576 | bytes 65536 | tf_op jit(solution)/shard_map/kern/pallas_call | solution.py:141
  25.4 0.0 copy-start.2
  25.5 3.3 %collective-permute-done.1.refs_0_.refs_1_ = bf16[1024,128]{1,0:T(8,128)(2,1)S(1)} collective-permute-done((bf16[1024,128]{1,0:T(8,128)(2,1)S(1)}, bf16[1024,128]{1,0:T(8,128)(2,1)S(1)}, u32[]{:S(2)}, u32[]{:S(2)}) %collective-permute-start.1) | collective-permute-done | bytes 262176 | tf_op jit(solution)/shard_map/ppermute | solution.py:293
  28.7 2.1 %kern.5.refs_0_ = bf16[1024,1024]{1,0:T(8,128)(2,1)S(1)} custom-call(f32[5,8,512]{2,1,0:T(8,128)S(1)} %cuts.1.cut_ref, bf16[1024,128]{1,0:T(8,128)(2,1)S(1)} %collective-permute-done.query_ref, bf16[1024,128]{1,0:T(8,128)(2,1)S(1)} %collective-permute-done.1.refs_0_.refs_1_), custom_call_target="tpu_custom_call" | custom-call | flops 1048576 | bytes 65536 | tf_op jit(solution)/shard_map/kern/pallas_call | solution.py:141
  30.8 0.0 copy-done.2
  30.8 1.3 %collective-permute-start.6 = (bf16[1024,1024]{1,0:T(8,128)(2,1)S(1)}, bf16[1024,1024]{1,0:T(8,128)(2,1)S(1)}, u32[]{:S(2)}, u32[]{:S(2)}) collective-permute-start(bf16[1024,1024]{1,0:T(8,128)(2,1)S(1)} %copy-done.2), channel_id=1, source_target_pairs={{4,12},{6,14},{8,0},{10,2},{12,20},{14,22},{16,8},{18,10},{20,28},... | collective-permute-start | bytes 6291464 | tf_op jit(solution)/shard_map/ppermute | solution.py:293
  32.1 2.6 %collective-permute-done.2.refs_1_.refs_3_ = bf16[1024,1024]{1,0:T(8,128)(2,1)S(1)} collective-permute-done((bf16[1024,1024]{1,0:T(8,128)(2,1)}, bf16[1024,1024]{1,0:T(8,128)(2,1)S(1)}, u32[]{:S(2)}, u32[]{:S(2)}) %collective-permute-start.2) | collective-permute-done | bytes 2097184 | tf_op jit(solution)/shard_map/ppermute | solution.py:293
  34.7 1.8 %scores.2 = bf16[1024,640]{1,0:T(8,128)(2,1)S(1)} custom-call(bf16[1024,1024]{1,0:T(8,128)(2,1)S(1)} %kern.5.refs_0_, bf16[1024,1024]{1,0:T(8,128)(2,1)S(1)} %collective-permute-done.2.refs_1_.refs_3_, bf16[1024,1024]{1,0:T(8,128)(2,1)S(1)} %kern.4.refs_2_), custom_call_target="tpu_custom_call" | custom-call | flops 1048576 | bytes 65536 | tf_op jit(solution)/shard_map/scores/pallas_call | solution.py:184
  36.5 0.0 copy-start
  36.5 4.2 %collective-permute-start.7 = (bf16[1024,640]{1,0:T(8,128)(2,1)S(1)}, bf16[1024,640]{1,0:T(8,128)(2,1)S(1)}, u32[]{:S(2)}, u32[]{:S(2)}) collective-permute-start(bf16[1024,640]{1,0:T(8,128)(2,1)S(1)} %scores.2), channel_id=1, source_target_pairs={{0,8},{1,5},{2,10},{3,7},{5,1},{7,3},{8,16},{9,13},{10,18},{11,15}... | collective-permute-start | bytes 3932168 | tf_op jit(solution)/shard_map/ppermute | solution.py:293
  40.7 0.7 collective-permute-start.4
  41.4 0.0 collective-permute-done.4.refs_1_
  41.4 0.0 collective-permute-done.3.refs_4_
  41.4 1.3 %scores.3 = bf16[1024,384]{1,0:T(8,128)(2,1)S(1)} custom-call(bf16[1024,1024]{1,0:T(8,128)(2,1)S(1)} %kern.5.refs_0_, bf16[1024,1024]{1,0:T(8,128)(2,1)S(1)} %collective-permute-done.2.refs_1_.refs_3_, bf16[1024,1024]{1,0:T(8,128)(2,1)S(1)} %kern.4.refs_2_), custom_call_target="tpu_custom_call" | custom-call | flops 1048576 | bytes 65536 | tf_op jit(solution)/shard_map/scores/pallas_call | solution.py:184
  42.7 3.5 %collective-permute-start.8 = (bf16[1024,384]{1,0:T(8,128)(2,1)S(1)}, bf16[1024,384]{1,0:T(8,128)(2,1)S(1)}, u32[]{:S(2)}, u32[]{:S(2)}) collective-permute-start(bf16[1024,384]{1,0:T(8,128)(2,1)S(1)} %scores.3), channel_id=1, source_target_pairs={{0,8},{1,5},{2,10},{3,7},{5,1},{7,3},{8,16},{9,13},{10,18},{11,15}... | collective-permute-start | bytes 2359304 | tf_op jit(solution)/shard_map/ppermute | solution.py:293
  46.1 1.5 %collective-permute-start.5 = (bf16[1024,128]{1,0:T(8,128)(2,1)S(1)}, bf16[1024,128]{1,0:T(8,128)(2,1)S(1)}, u32[]{:S(2)}, u32[]{:S(2)}) collective-permute-start(bf16[1024,128]{1,0:T(8,128)(2,1)S(1)} %collective-permute-done.1.refs_0_.refs_1_), channel_id=1, source_target_pairs={{1,0},{3,2},{5,4},{7,6},{9,8},{11,10},{13,12},{15,14},{17,16},{19,... | collective-permute-start | bytes 786440 | tf_op jit(solution)/shard_map/ppermute | solution.py:293
  47.6 0.0 copy-done
  47.6 7.9 %kern.6 = (f32[1024,1024]{1,0:T(8,128)S(1)}, bf16[1024,1024]{1,0:T(8,128)(2,1)S(1)}) custom-call(f32[5,8,512]{2,1,0:T(8,128)S(1)} %cuts.1.cut_ref, bf16[1024,128]{1,0:T(8,128)(2,1)S(1)} %copy-done, bf16[1024,128]{1,0:T(8,128)(2,1)S(1)} %all_gather.3.refs_0_, bf16[1024,128]{1,0:T(8,128)(2,1)S(1)} %collective-permute-done.1.refs_0_.refs_1_, ...), custom_call_target="tpu_custom_call" | custom-call | flops 1048576 | bytes 65536 | tf_op jit(solution)/shard_map/kern/pallas_call | solution.py:141
  55.5 0.0 collective-permute-done.5.refs_0_
  55.5 2.0 %kern.7.kern_ref = bf16[1024,1024]{1,0:T(8,128)(2,1)S(1)} custom-call(f32[5,8,512]{2,1,0:T(8,128)S(1)} %cuts.1.cut_ref, bf16[1024,128]{1,0:T(8,128)(2,1)S(1)} %copy-done, bf16[1024,128]{1,0:T(8,128)(2,1)S(1)} %collective-permute-done.5.refs_0_, bf16[1024,128]{1,0:T(8,128)(2,1)S(1)} %collective-permute-done.4.refs_1_), custom_call_target="tpu_custom_call" | custom-call | flops 1048576 | bytes 65536 | tf_op jit(solution)/shard_map/kern/pallas_call | solution.py:141
  57.6 1.1 %collective-permute-done.6.far_0_ref = bf16[1024,1024]{1,0:T(8,128)(2,1)S(1)} collective-permute-done((bf16[1024,1024]{1,0:T(8,128)(2,1)S(1)}, bf16[1024,1024]{1,0:T(8,128)(2,1)S(1)}, u32[]{:S(2)}, u32[]{:S(2)}) %collective-permute-start.6) | collective-permute-done | bytes 2097184 | tf_op jit(solution)/shard_map/ppermute | solution.py:293
  58.7 0.0 collective-permute-done.7.part_ref
  58.7 3.8 %far.1 = (bf16[1024,1024]{1,0:T(8,128)(2,1)}, f32[1024,384]{1,0:T(8,128)S(1)}) custom-call(s32[2]{0:T(128)S(1)} %pad_add_fusion.place_ref, bf16[1024,1024]{1,0:T(8,128)(2,1)S(1)} %kern.7.kern_ref, bf16[1024,1024]{1,0:T(8,128)(2,1)S(1)} %collective-permute-done.6.far_0_ref, bf16[1024,1024]{1,0:T(8,128)(2,1)S(1)} %get-tuple-element.28.far_1_ref, ...), custom_call_target="tpu_custom_call" | custom-call | flops 1048576 | bytes 65536 | tf_op jit(solution)/shard_map/far/pallas_call | solution.py:228
  62.6 4.4 %collective-permute-done.8.part_ref = bf16[1024,384]{1,0:T(8,128)(2,1)S(1)} collective-permute-done((bf16[1024,384]{1,0:T(8,128)(2,1)S(1)}, bf16[1024,384]{1,0:T(8,128)(2,1)S(1)}, u32[]{:S(2)}, u32[]{:S(2)}) %collective-permute-start.8) | collective-permute-done | bytes 786464 | tf_op jit(solution)/shard_map/ppermute | solution.py:293
  67.0 1.0 %final.1 = bf16[1024,1024]{1,0:T(8,128)(2,1)} custom-call(f32[1024,384]{1,0:T(8,128)S(1)} %get-tuple-element.29.add_ref, bf16[1024,384]{1,0:T(8,128)(2,1)S(1)} %collective-permute-done.8.part_ref, bf16[1024,1024]{1,0:T(8,128)(2,1)} %get-tuple-element.30._), custom_call_target="tpu_custom_call", output_to_operand_aliasing={{}: (2, {})} | custom-call | flops 1048576 | bytes 65536 | tf_op jit(solution)/shard_map/final/pallas_call | solution.py:260
Async XLA Ops:
  0.0 34.7 %collective-permute-start.2 = (bf16[1024,1024]{1,0:T(8,128)(2,1)}, bf16[1024,1024]{1,0:T(8,128)(2,1)S(1)}, u32[]{:S(2)}, u32[]{:S(2)}) collective-permute-start(bf16[1024,1024]{1,0:T(8,128)(2,1)} %refs_2_.1), channel_id=1, source_target_pairs={{0,4},{2,6},{4,0},{5,13},{6,2},{7,15},{8,12},{9,1},{10,14},{11,3},... | collective-permute-start | bytes 6291464 | tf_op jit(solution)/shard_map/ppermute | solution.py:293
  4.8 36.6 %collective-permute-start.3 = (bf16[1024,1024]{1,0:T(8,128)(2,1)}, bf16[1024,1024]{1,0:T(8,128)(2,1)}, u32[]{:S(2)}, u32[]{:S(2)}) collective-permute-start(bf16[1024,1024]{1,0:T(8,128)(2,1)} %refs_2_.1), channel_id=1, source_target_pairs={{1,9},{3,11},{9,17},{11,19},{13,5},{15,7},{17,25},{19,27},{21,13},... | collective-permute-start | bytes 6291464 | tf_op jit(solution)/shard_map/ppermute | solution.py:293
  6.8 11.3 %collective-permute-start = (bf16[1024,128]{1,0:T(8,128)(2,1)}, bf16[1024,128]{1,0:T(8,128)(2,1)S(1)}, u32[]{:S(2)}, u32[]{:S(2)}) collective-permute-start(bf16[1024,128]{1,0:T(8,128)(2,1)} %query_ref.3), channel_id=1, source_target_pairs={{1,5},{3,7},{4,12},{5,1},{6,14},{7,3},{8,0},{9,13},{10,2},{11,15},... | collective-permute-start | bytes 786440 | tf_op jit(solution)/shard_map/ppermute | solution.py:293
  18.2 10.6 %collective-permute-start.1 = (bf16[1024,128]{1,0:T(8,128)(2,1)S(1)}, bf16[1024,128]{1,0:T(8,128)(2,1)S(1)}, u32[]{:S(2)}, u32[]{:S(2)}) collective-permute-start(bf16[1024,128]{1,0:T(8,128)(2,1)S(1)} %all_gather.3.refs_0_), channel_id=1, source_target_pairs={{1,4},{3,6},{4,13},{5,0},{6,15},{7,2},{8,1},{9,12},{10,3},{11,14},... | collective-permute-start | bytes 786440 | tf_op jit(solution)/shard_map/ppermute | solution.py:293
  19.5 0.7 %copy-start.1 = (s32[8,5]{1,0:T(8,128)S(1)}, s32[8,5]{1,0:T(8,128)}, u32[]{:S(2)}) copy-start(s32[8,5]{1,0:T(8,128)} %pattern_ref.1) | copy-start | bytes 484
  25.4 5.4 %copy-start.2 = (bf16[1024,1024]{1,0:T(8,128)(2,1)S(1)}, bf16[1024,1024]{1,0:T(8,128)(2,1)}, u32[]{:S(2)}) copy-start(bf16[1024,1024]{1,0:T(8,128)(2,1)} %refs_2_.1) | copy-start | bytes 6291460
  30.8 27.9 %collective-permute-start.6 = (bf16[1024,1024]{1,0:T(8,128)(2,1)S(1)}, bf16[1024,1024]{1,0:T(8,128)(2,1)S(1)}, u32[]{:S(2)}, u32[]{:S(2)}) collective-permute-start(bf16[1024,1024]{1,0:T(8,128)(2,1)S(1)} %copy-done.2), channel_id=1, source_target_pairs={{4,12},{6,14},{8,0},{10,2},{12,20},{14,22},{16,8},{18,10},{20,28},... | collective-permute-start | bytes 6291464 | tf_op jit(solution)/shard_map/ppermute | solution.py:293
  36.5 11.1 %copy-start = (bf16[1024,128]{1,0:T(8,128)(2,1)S(1)}, bf16[1024,128]{1,0:T(8,128)(2,1)}, u32[]{:S(2)}) copy-start(bf16[1024,128]{1,0:T(8,128)(2,1)} %query_ref.3) | copy-start | bytes 786436
  36.5 22.3 %collective-permute-start.7 = (bf16[1024,640]{1,0:T(8,128)(2,1)S(1)}, bf16[1024,640]{1,0:T(8,128)(2,1)S(1)}, u32[]{:S(2)}, u32[]{:S(2)}) collective-permute-start(bf16[1024,640]{1,0:T(8,128)(2,1)S(1)} %scores.2), channel_id=1, source_target_pairs={{0,8},{1,5},{2,10},{3,7},{5,1},{7,3},{8,16},{9,13},{10,18},{11,15}... | collective-permute-start | bytes 3932168 | tf_op jit(solution)/shard_map/ppermute | solution.py:293
  40.7 0.7 %collective-permute-start.4 = (bf16[1024,128]{1,0:T(8,128)(2,1)S(1)}, bf16[1024,128]{1,0:T(8,128)(2,1)S(1)}, u32[]{:S(2)}, u32[]{:S(2)}) collective-permute-start(bf16[1024,128]{1,0:T(8,128)(2,1)S(1)} %all_gather.3.refs_0_), channel_id=1, source_target_pairs={{1,9},{3,11},{9,17},{11,19},{13,5},{15,7},{17,25},{19,27},{21,13},... | collective-permute-start | bytes 786440 | tf_op jit(solution)/shard_map/ppermute | solution.py:293
  42.7 24.3 %collective-permute-start.8 = (bf16[1024,384]{1,0:T(8,128)(2,1)S(1)}, bf16[1024,384]{1,0:T(8,128)(2,1)S(1)}, u32[]{:S(2)}, u32[]{:S(2)}) collective-permute-start(bf16[1024,384]{1,0:T(8,128)(2,1)S(1)} %scores.3), channel_id=1, source_target_pairs={{0,8},{1,5},{2,10},{3,7},{5,1},{7,3},{8,16},{9,13},{10,18},{11,15}... | collective-permute-start | bytes 2359304 | tf_op jit(solution)/shard_map/ppermute | solution.py:293
  46.1 9.4 %collective-permute-start.5 = (bf16[1024,128]{1,0:T(8,128)(2,1)S(1)}, bf16[1024,128]{1,0:T(8,128)(2,1)S(1)}, u32[]{:S(2)}, u32[]{:S(2)}) collective-permute-start(bf16[1024,128]{1,0:T(8,128)(2,1)S(1)} %collective-permute-done.1.refs_0_.refs_1_), channel_id=1, source_target_pairs={{1,0},{3,2},{5,4},{7,6},{9,8},{11,10},{13,12},{15,14},{17,16},{19,... | collective-permute-start | bytes 786440 | tf_op jit(solution)/shard_map/ppermute | solution.py:293
